TPU v7x, 512 devices: a whole 4x4x16 slice. The times are simulated.
512 devices in a mesh: ctx: 128 (over y, z, x_hi), grp: 4 (over x_lo, core).
Axes of the slice: x: 4 (x_hi: 2, x_lo: 2; x = x_hi * 2 + x_lo), y: 4, z: 16, core: 2. Of those that a mesh axis runs over, the one named last changes fastest.
Arguments:
- queries: bfloat16 [2048, 6144], P('ctx'), may hold values from -9 to 9
- keys: bfloat16 [30720, 512], P(('ctx', 'grp')), may hold values from -6 to 6
- values: bfloat16 [30720, 512], P(('ctx', 'grp')), may hold values from -6 to 6
- own_keys: bfloat16 [2048, 512], P('ctx', 'grp'), may hold values from -12 to 12
- own_values: bfloat16 [2048, 512], P('ctx', 'grp'), may hold values from -6 to 6
Outputs:
- attended: bfloat16 [2048, 6144], P('ctx', 'grp')
All inputs are finite; a program needn't handle non-finite values.
Results may differ from a plain program's by a relative error of at most 0.0055.
Values may be sent and summed in bfloat16 or wider, within the bound.
A program may use at most 64 MiB of HBM per device.

v0:
```python
import jax
import jax.numpy as jnp
from jax import lax
from jax.sharding import PartitionSpec as P

HS = 128
KVH = 4
HQ = 48


def shifted(x, axis, by):
    count = lax.axis_size(axis)
    return lax.ppermute(x, axis, [(i, (i + by) % count) for i in range(count)])


def joined(x, axis, combine):
    everything = jax.tree.map(lambda part: lax.all_gather(part, axis), x)
    initial = jax.tree.map(lambda part: part[0], everything)

    def joined_turn(k, so_far):
        return combine(so_far, jax.tree.map(lambda part: part[k], everything))

    return lax.fori_loop(1, lax.axis_size(axis), joined_turn, initial)


def absorb(carried, pair_block, query_heads, score_scale):
    maxima, totals, running = carried
    key_count = pair_block.shape[1]
    head_count = query_heads.shape[0]
    block_keys = pair_block[0].reshape(key_count, head_count, -1)
    block_values = pair_block[1].reshape(key_count, head_count, -1)
    scores = (
        jnp.einsum("kgh,grh->gkr", block_keys, query_heads, preferred_element_type=jnp.float32)
        * score_scale
    )
    new_max = jnp.maximum(maxima, jnp.max(scores, axis=1))
    factor = jnp.exp(maxima - new_max)
    weights = jnp.exp(scores - new_max[:, None, :])
    totals = totals * factor + jnp.sum(weights, axis=1)
    running = running * factor[..., None] + jnp.einsum(
        "gkr,kgh->grh",
        weights.astype(jnp.bfloat16),
        block_values,
        preferred_element_type=jnp.float32,
    )
    return (new_max, totals, running)


def combine(first, second):
    new_max = jnp.maximum(first[0], second[0])
    first_factor = jnp.exp(first[0] - new_max)
    second_factor = jnp.exp(second[0] - new_max)
    totals = first[1] * first_factor + second[1] * second_factor
    running = first[2] * first_factor[..., None] + second[2] * second_factor[..., None]
    return (new_max, totals, running)


def local(queries, keys, values, own_keys, own_values):
    row_count = queries.shape[0]
    group_size = HQ // KVH
    score_scale = HS ** (-0.5)
    query_heads = (
        queries.reshape(row_count, KVH, group_size, HS)
        .transpose(1, 2, 0, 3)
        .reshape(KVH, group_size * row_count, HS)
    )
    group_count = lax.axis_size("grp")
    my_index = lax.axis_index("grp")
    per_device = KVH // group_count
    start_head = my_index * per_device
    mine_queries = lax.dynamic_slice_in_dim(query_heads, start_head, per_device, 0)
    own_key_rows = jnp.tile(
        own_keys.reshape(row_count, per_device, HS).transpose(1, 0, 2), (1, group_size, 1)
    )
    own_value_rows = jnp.tile(
        own_values.reshape(row_count, per_device, HS).transpose(1, 0, 2), (1, group_size, 1)
    )
    own_scores = (
        jnp.sum(mine_queries.astype(jnp.float32) * own_key_rows.astype(jnp.float32), axis=-1)
        * score_scale
    )
    maxima = jnp.full((KVH, group_size * row_count), -1e30, jnp.float32)
    maxima = lax.dynamic_update_slice_in_dim(maxima, own_scores, start_head, 0)
    totals = jnp.zeros((KVH, group_size * row_count), jnp.float32)
    totals = lax.dynamic_update_slice_in_dim(totals, jnp.ones_like(own_scores), start_head, 0)
    running = jnp.zeros((KVH, group_size * row_count, HS), jnp.float32)
    running = lax.dynamic_update_slice_in_dim(
        running, own_value_rows.astype(jnp.float32), start_head, 0
    )
    pairs = jnp.stack([keys, values])
    carried = absorb((maxima, totals, running), pairs, query_heads, score_scale)
    cycle_length = lax.axis_size("ctx")

    def body_turn(turn_index, loop_state):
        moving, inner = loop_state
        moving = shifted(moving, "ctx", 1)
        return (moving, absorb(inner, moving, query_heads, score_scale))

    pairs, carried = lax.fori_loop(1, cycle_length, body_turn, (pairs, carried))
    maxima, totals, running = carried
    maxima, totals, running = joined((maxima, totals, running), "grp", combine)
    totals = lax.dynamic_slice_in_dim(totals, start_head, per_device, 0)
    running = lax.dynamic_slice_in_dim(running, start_head, per_device, 0)
    outcome = running / totals[..., None]
    outcome = outcome.reshape(per_device, group_size, row_count, HS).transpose(2, 0, 1, 3)
    return outcome.reshape(row_count, per_device * group_size * HS).astype(jnp.bfloat16)


def solution(mesh):
    placed = (
        P("ctx", None),
        P(("ctx", "grp"), None),
        P(("ctx", "grp"), None),
        P("ctx", "grp"),
        P("ctx", "grp"),
    )
    return jax.shard_map(
        local, mesh=mesh, in_specs=placed, out_specs=P("ctx", "grp"), check_vma=False
    )
```

profile of v0, /device:TPU:1, one launch (start us, length us, event | category | flops | bytes accessed | tf_op | source)
XLA Modules:
  0.0 1771.7 jit_solution(4084070569705318051)
XLA Ops:
  10.7 1586.5 %while.35 = (s32[]{:T(128)}, bf16[2,60,512]{2,1,0:T(8,128)(2,1)S(1)}, f32[4,192]{1,0:T(4,128)S(1)}, f32[4,192]{1,0:T(4,128)S(1)}, f32[4,192,128]{2,1,0:T(8,128)S...) while((s32[]{:T(128)}, bf16[2,60,512]{2,1,0:T(8,128)(2,1)S(1)}, f32[4,192]{1,0:T(4,128)S(1)}, ...), condition=%wide.region_6.0_spmd, body=%wide.region_3.0_spmd.sunk | while | flops 24067584 | bytes 2936949 | solution.py:99
  16.2 14.6 collective-permute-done
  33.5 9.5 collective-permute-done
  45.8 9.5 collective-permute-done
  58.0 9.5 collective-permute-done
  70.3 9.5 collective-permute-done
  82.5 9.5 collective-permute-done
  94.8 9.5 collective-permute-done
  107.0 9.5 collective-permute-done
  143.8 9.6 collective-permute-done
  156.1 10.7 collective-permute-done
  169.6 10.4 collective-permute-done
  256.2 9.5 collective-permute-done
  293.0 9.6 collective-permute-done
  305.3 10.7 collective-permute-done
  318.8 10.4 collective-permute-done
  393.2 9.5 collective-permute-done
  442.2 9.6 collective-permute-done
  454.5 10.7 collective-permute-done
  468.0 10.4 collective-permute-done
  591.4 9.6 collective-permute-done
  603.7 10.7 collective-permute-done
  617.2 10.4 collective-permute-done
  691.6 9.5 collective-permute-done
  740.6 9.6 collective-permute-done
  752.9 10.7 collective-permute-done
  766.4 10.4 collective-permute-done
  828.5 9.5 collective-permute-done
  889.8 9.6 collective-permute-done
  902.1 10.7 collective-permute-done
  915.6 10.4 collective-permute-done
  1039.0 9.6 collective-permute-done
  1051.3 10.7 collective-permute-done
  1064.8 10.4 collective-permute-done
  1126.9 9.5 collective-permute-done
  1188.2 9.6 collective-permute-done
  1200.5 10.7 collective-permute-done
  1214.0 10.4 collective-permute-done
  1263.9 9.5 collective-permute-done
  1337.4 9.6 collective-permute-done
  1349.7 10.7 collective-permute-done
  1363.2 10.4 collective-permute-done
  1486.6 9.6 collective-permute-done
  1498.9 10.7 collective-permute-done
  1512.4 10.4 collective-permute-done
  1562.3 9.5 collective-permute-done
  1586.8 9.6 collective-permute-done
  1597.9 147.2 %all-gather.4 = f32[4,4,192]{2,1,0:T(4,128)S(1)} all-gather(f32[1,4,192]{2,1,0:T(4,128)S(1)} %bitcast.62), channel_id=3, replica_groups=mesh['ctx'=128,'grp'=4] {'grp'}, dimensions={0}, use_global_device_ids=true | all-gather | bytes 15360 | tf_op jit(solution)/shard_map/all_gather | solution.py:17
  (1526 shorter events, 1141.8 us)
Async XLA Ops:
  6.5 1752.2 %all-gather.7.cloned.1.call-start = ((), (), s32[]{:S(2)}) async-start(), calls=%async_computation | async-start | bytes 1966080 | tf_op jit(solution)/shard_map/all_gather | solution.py:17
  10.7 20.1 %collective-permute-start = (bf16[2,60,512]{2,1,0:T(8,128)(2,1)S(1)}, bf16[2,60,512]{2,1,0:T(8,128)(2,1)S(1)}, u32[]{:S(2)}, u32[]{:S(2)}) collective-permute-start(bf16[2,60,512]{2,1,0:T(8,128)(2,1)S(1)} %get-tuple-element.371), channel_id=1, source_target_pairs={{0,4},{4,8},{8,12},{12,16},{16,20},{20,24},{24,28},{28,32},{32,36}... | collective-permute-start | bytes 368648 | tf_op jit(solution)/shard_map/while/body/eval_jaxpr/ppermute | solution.py:13
  31.6 11.4 collective-permute-start
  43.8 11.4 collective-permute-start
  56.1 11.4 collective-permute-start
  117.3 11.4 collective-permute-start
  141.8 11.5 collective-permute-start
  154.2 12.7 collective-permute-start
  167.7 12.3 collective-permute-start
  254.3 11.4 collective-permute-start
  291.0 11.5 collective-permute-start
  303.4 12.7 collective-permute-start
  316.9 12.3 collective-permute-start
  330.0 11.4 collective-permute-start
  391.2 11.4 collective-permute-start
  440.3 11.5 collective-permute-start
  452.6 12.7 collective-permute-start
  466.1 12.3 collective-permute-start
  552.7 11.4 collective-permute-start
  589.5 11.5 collective-permute-start
  601.8 12.7 collective-permute-start
  615.3 12.3 collective-permute-start
  689.7 11.4 collective-permute-start
  738.7 11.5 collective-permute-start
  751.0 12.7 collective-permute-start
  764.5 12.3 collective-permute-start
  826.6 11.4 collective-permute-start
  887.9 11.5 collective-permute-start
  900.2 12.7 collective-permute-start
  913.7 12.3 collective-permute-start
  988.1 11.4 collective-permute-start
  1037.1 11.5 collective-permute-start
  1049.4 12.7 collective-permute-start
  1062.9 12.3 collective-permute-start
  1125.0 11.4 collective-permute-start
  1186.3 11.5 collective-permute-start
  1198.6 12.7 collective-permute-start
  1212.1 12.3 collective-permute-start
  1262.0 11.4 collective-permute-start
  1335.5 11.5 collective-permute-start
  1347.8 12.7 collective-permute-start
  1361.3 12.3 collective-permute-start
  1423.4 11.4 collective-permute-start
  1484.7 11.5 collective-permute-start
  1497.0 12.7 collective-permute-start
  1510.5 12.3 collective-permute-start
  1560.4 11.4 collective-permute-start
  1584.9 11.5 collective-permute-start
  (85 other events, 929.4 us)
Sparse Core Ops, SparseCore 0:
  1598.1 160.6 all-gather.6
where the time goes:
time: 1780 us; the launch traced here: 1770 us
  waiting for transfers between devices  1240 us (70%)
  starting transfers between devices  248 us (14%)
  blocking collectives  152 us (9%)
  matrix products  76.8 us (4%)
    ppermute x127, waiting for transfers between devices, shifted(): return lax.ppermute(x, axis, [(i, (i + by) % count) for i in range(count)])  1230 us
    ppermute x127, starting transfers between devices, shifted(): return lax.ppermute(x, axis, [(i, (i + by) % count) for i in range(count)])  247 us
    all_gather x2, blocking collectives, joined(): everything = jax.tree.map(lambda part: lax.all_gather(part, axis), x)  152 us
    dot_general x128, matrix products, absorb(): jnp.einsum('gkr,kgh->grh', weights.astype(jnp.bfloat16), block_values, pr...  43.1 us
  transfers between devices with their start and end apart: 128, of which 128 were waited for; matrix products, arithmetic and copies ran while one was open for 0% of the time, Pallas kernels for 0%

commit v1 on v0

v1 whole, which is shorter than its diff:
```python
import functools
import math

import jax
import jax.numpy as jnp
from jax import lax
from jax.experimental import pallas as pl
from jax.experimental.pallas import tpu as pltpu
from jax.sharding import PartitionSpec as P

MESH = pl.DeviceIdType.MESH
HS = 128
KVH = 4
GROUP = 12
ROWS = 16
XS, YS, ZS = 4, 4, 16
KEYS = 60
PAD = 64
HALF = ZS // 2
SLOTS = ZS
SCALE = math.log2(math.e) / math.sqrt(HS)
QB = GROUP * ROWS
LANES = 16


def device(x, y, z, c):
    return {"ctx": (y * ZS + z) * 2 + x // 2, "grp": lax.rem(x, 2) * 2 + c}


def head_of(x):
    return x // 2 + 2 * (1 - lax.rem(x, 2))


def nt(a, b):
    return lax.dot_general(a, b, (((1,), (1,)), ((), ())), preferred_element_type=jnp.float32)


def kernel(
    q_ref, k_ref, v_ref, ok_ref, ov_ref, out_ref,
    pad32, kvst, qs, qbuf, kv, sib, acc, top, own, omsg, orecv,
    first_send, ring_send, ring_recv, sib_send, sib_recv, q_send, q_recv, o_send, o_recv,
):
    ctx, grp = lax.axis_index("ctx"), lax.axis_index("grp")
    xhi, z, y = lax.rem(ctx, 2), lax.rem(ctx // 2, ZS), ctx // (2 * ZS)
    xlo, c = grp // 2, lax.rem(grp, 2)
    x = 2 * xhi + xlo
    mine = head_of(x)

    def at_x(dx):
        return lax.rem(x + dx, XS)

    def at_y(dy):
        return lax.rem(y + dy, YS)

    z_next = (lax.rem(z + 1, ZS), lax.rem(z + ZS - 1, ZS), z)
    sibling = device(x, y, z, 1 - c)
    q_x = jnp.where(c == 0, x, XS - 1 - x)
    q_self = jnp.logical_and(c == 0, xhi == 0)
    q_from_own = c == xhi
    q_from_x = jnp.where(q_from_own, x, XS - 1 - x)
    q_from_c = jnp.where(q_from_own, 0, 1)
    o_x, o_c = 2 * c + mine // 2, lax.rem(mine, 2)
    o_from_x, o_from_c = 2 * c + 1 - xlo, xhi

    barrier = pltpu.get_barrier_semaphore()

    def greet(to):
        pl.semaphore_signal(barrier, inc=1, device_id=to, device_id_type=MESH)

    for dz in (0, 1):
        for dx in range(XS):
            greet(device(at_x(dx), y, z_next[dz], c))
    for dx in range(1, XS):
        greet(device(at_x(dx), y, z, c))
    greet(sibling)
    for dy in range(YS):
        greet(device(o_from_x, at_y(dy), z, o_from_c))
        if dy:
            greet(device(q_from_x, at_y(dy), z, q_from_c))

    @pl.when(jnp.logical_not(q_self))
    def _():
        greet(device(q_from_x, y, z, q_from_c))

    for which, ref in ((0, k_ref), (1, v_ref)):
        rows = ref[...].astype(jnp.float32)
        pad32[0:KEYS, :] = rows
        if which == 0:
            pad32[KEYS:PAD, :] = rows[0 : PAD - KEYS, :]
        else:
            pad32[KEYS:PAD, :] = jnp.zeros((PAD - KEYS, KVH * HS), jnp.float32)
        for h in range(KVH):
            kvst[h, which] = pad32[:, h * HS : (h + 1) * HS].astype(jnp.bfloat16)
    for h in range(KVH * GROUP):
        qs[h] = q_ref[:, h * HS : (h + 1) * HS]

    expected = 2 * XS + XS - 1 + 1 + 2 * YS - 1
    pl.semaphore_wait(barrier, jnp.where(q_self, expected, expected + 1))

    def first(dz, dx):
        to = at_x(dx)
        slot = (1, 2, 0)[dz]
        return pltpu.make_async_remote_copy(
            src_ref=kvst.at[head_of(to)],
            dst_ref=kv.at[slot, x],
            send_sem=first_send.at[dz, dx],
            recv_sem=ring_recv.at[slot, x],
            device_id=device(to, y, z_next[dz], c),
            device_id_type=MESH,
        )

    def query(dy):
        return pltpu.make_async_remote_copy(
            src_ref=qs.at[pl.ds(head_of(q_x) * GROUP, GROUP)],
            dst_ref=qbuf.at[(YS - dy) % YS],
            send_sem=q_send.at[dy],
            recv_sem=q_recv.at[(YS - dy) % YS],
            device_id=device(q_x, at_y(dy), z, xhi),
            device_id_type=MESH,
        )

    for dx in (2, 1, 3, 0):
        for dz in (0, 1):
            first(dz, dx).start()
    for dx in (2, 1, 3):
        first(2, dx).start()
    for dy in (2, 1, 3):
        query(dy).start()

    @pl.when(jnp.logical_not(q_self))
    def _():
        query(0).start()

    @pl.when(q_self)
    def _():
        qbuf[0] = qs[pl.ds(mine * GROUP, GROUP)]

    kv[0, x] = kvst[mine]

    def forward(d, slot, to_slot, piece):
        return pltpu.make_async_remote_copy(
            src_ref=kv.at[slot, piece],
            dst_ref=kv.at[to_slot, piece],
            send_sem=ring_send.at[slot, piece],
            recv_sem=ring_recv.at[to_slot, piece],
            device_id=device(x, y, z_next[d], c),
            device_id_type=MESH,
        )

    def arrived(d, slot, piece):
        forward(d, slot, slot, piece).wait_recv()

    def across(slot):
        return pltpu.make_async_remote_copy(
            src_ref=kv.at[slot],
            dst_ref=sib.at[slot],
            send_sem=sib_send.at[slot],
            recv_sem=sib_recv.at[slot],
            device_id=sibling,
            device_id_type=MESH,
        )

    lane = lax.broadcasted_iota(jnp.int32, (ROWS, HS), 1)
    own_scores = jnp.zeros((ROWS, HS), jnp.float32)
    group = 2 * xlo + c
    own_key = ok_ref[...].astype(jnp.float32)
    for h in range(GROUP):
        product = qs[group * GROUP + h].astype(jnp.float32) * own_key
        score = jnp.sum(product, axis=1, keepdims=True) * SCALE
        own_scores = jnp.where(lane == h, score, own_scores)
    own[...] = own_scores

    top[...] = jnp.full(top.shape, -1e30, jnp.float32)
    acc[...] = jnp.zeros(acc.shape, jnp.float32)
    real = lax.broadcasted_iota(jnp.int32, (8, PAD, HS), 1) < KEYS
    ones = jnp.where(real, 1.0, 0.0).astype(jnp.bfloat16).reshape(8 * PAD, HS)

    def block_of(slot):
        keys = jnp.concatenate(
            [kv[slot, :, 0].reshape(4 * PAD, HS), sib[slot, :, 0].reshape(4 * PAD, HS)], axis=0
        )
        values = jnp.concatenate(
            [kv[slot, :, 1].reshape(4 * PAD, HS), sib[slot, :, 1].reshape(4 * PAD, HS)], axis=0
        )
        return keys, jnp.concatenate([values, ones], axis=1)

    def absorb(i, keys, values):
        scores = nt(qbuf[i].reshape(QB, HS), keys) * SCALE
        before = top[i][:, :1]
        best = jnp.max(scores, axis=1, keepdims=True).astype(jnp.bfloat16).astype(jnp.float32)
        now = jnp.maximum(before, best)
        weights = jnp.exp2(scores - now).astype(jnp.bfloat16)
        mixed = jnp.dot(weights, values, preferred_element_type=jnp.float32)
        acc[i] = acc[i] * jnp.exp2(before - now) + mixed
        top[i] = jnp.broadcast_to(now, (QB, HS))

    def compute(slot):
        across(slot).wait_recv()
        keys, values = block_of(slot)

        def turn(i, _):
            absorb(i, keys, values)
            return 0

        lax.fori_loop(0, YS, turn, 0)

    for dx in (1, 2, 3):
        arrived(0, 0, at_x(dx))
    across(0).start()
    for dy in (1, 2, 3):
        query(dy).wait_recv()

    @pl.when(jnp.logical_not(q_self))
    def _():
        query(0).wait_recv()

    def step(s, _):
        slot = 2 * s - 1
        for piece in range(XS):
            for d in (0, 1):
                arrived(d, slot + d, piece)
                forward(d, slot + d, slot + 2 + d, piece).start()
        for d in (0, 1):
            across(slot + d).start()
        compute(slot - 1)
        compute(slot)
        return 0

    lax.fori_loop(1, HALF - 1, step, 0)
    slot = 2 * HALF - 3
    for piece in range(XS):
        for d in (0, 1):
            arrived(d, slot + d, piece)
            if piece // 2 == d:
                forward(d, slot + d, SLOTS - 1, piece).start()
    for d in (0, 1):
        across(slot + d).start()
    compute(slot - 1)
    compute(slot)
    for piece in range(XS):
        arrived(piece // 2, SLOTS - 1, piece)
    across(SLOTS - 1).start()
    compute(SLOTS - 2)

    def result(dy):
        return pltpu.make_async_remote_copy(
            src_ref=omsg.at[dy],
            dst_ref=orecv.at[(YS - dy) % YS],
            send_sem=o_send.at[dy],
            recv_sem=o_recv.at[(YS - dy) % YS],
            device_id=device(o_x, at_y(dy), z, o_c),
            device_id_type=MESH,
        )

    across(SLOTS - 1).wait_recv()
    keys, values = block_of(SLOTS - 1)
    for dy in (2, 1, 3, 0):
        absorb(dy, keys, values)
        omsg[dy, 0:GROUP] = acc[dy, :, :HS].astype(jnp.bfloat16).reshape(GROUP, ROWS, HS)
        stats = jnp.zeros((ROWS, HS), jnp.float32)
        for h in range(GROUP):
            rows = slice(h * ROWS, (h + 1) * ROWS)
            total = acc[dy, rows, HS:]
            high = total.astype(jnp.bfloat16).astype(jnp.float32)
            stats = jnp.where(lane == h, top[dy, rows], stats)
            stats = jnp.where(lane == LANES + h, high, stats)
            stats = jnp.where(lane == 2 * LANES + h, total - high, stats)
        omsg[dy, GROUP] = stats.astype(jnp.bfloat16)
        result(dy).start()

    for dy in range(YS):
        result(dy).wait_recv()
    largest = own[...]
    tops, totals = [], []
    for i in range(YS):
        stats = orecv[i, GROUP].astype(jnp.float32)
        tops.append(stats)
        totals.append(pltpu.roll(stats, HS - LANES, 1) + pltpu.roll(stats, HS - 2 * LANES, 1))
        largest = jnp.maximum(largest, stats)
    own_factor = jnp.exp2(own[...] - largest)
    factors = [jnp.exp2(t - largest) for t in tops]
    total = own_factor
    for factor, part in zip(factors, totals):
        total = total + factor * part
    own_factor = own_factor / total
    factors = [factor / total for factor in factors]
    own_value = ov_ref[...].astype(jnp.float32)
    for h in range(GROUP):
        mixed = own_factor[:, h : h + 1] * own_value
        for i in range(YS):
            mixed = mixed + factors[i][:, h : h + 1] * orecv[i, h].astype(jnp.float32)
        out_ref[:, h * HS : (h + 1) * HS] = mixed.astype(jnp.bfloat16)

    for dz in range(3):
        for dx in range(XS):
            if dz < 2 or dx:
                first(dz, dx).wait_send()
    for dy in (1, 2, 3):
        query(dy).wait_send()

    @pl.when(jnp.logical_not(q_self))
    def _():
        query(0).wait_send()

    def sent(slot, _):
        for piece in range(XS):
            forward(0, slot, slot, piece).wait_send()
        return 0

    lax.fori_loop(1, SLOTS - 3, sent, 0)
    for piece in range(XS):
        forward(0, slot + piece // 2, SLOTS - 1, piece).wait_send()

    def crossed(slot, _):
        across(slot).wait_send()
        return 0

    lax.fori_loop(0, SLOTS, crossed, 0)
    for dy in range(YS):
        result(dy).wait_send()


def local(queries, keys, values, own_keys, own_values):
    vmem = pl.BlockSpec(memory_space=pltpu.VMEM)
    bf16, f32 = jnp.bfloat16, jnp.float32
    dma = pltpu.SemaphoreType.DMA
    return pl.pallas_call(
        kernel,
        out_shape=jax.ShapeDtypeStruct((ROWS, GROUP * HS), bf16),
        in_specs=[vmem] * 5,
        out_specs=vmem,
        scratch_shapes=[
            pltpu.VMEM((PAD, KVH * HS), f32),
            pltpu.VMEM((KVH, 2, PAD, HS), bf16),
            pltpu.VMEM((KVH * GROUP, ROWS, HS), bf16),
            pltpu.VMEM((YS, GROUP, ROWS, HS), bf16),
            pltpu.VMEM((SLOTS, XS, 2, PAD, HS), bf16),
            pltpu.VMEM((SLOTS, XS, 2, PAD, HS), bf16),
            pltpu.VMEM((YS, QB, 2 * HS), f32),
            pltpu.VMEM((YS, QB, HS), f32),
            pltpu.VMEM((ROWS, HS), f32),
            pltpu.VMEM((YS, GROUP + 1, ROWS, HS), bf16),
            pltpu.VMEM((YS, GROUP + 1, ROWS, HS), bf16),
            dma((3, XS)),
            dma((SLOTS, XS)),
            dma((SLOTS, XS)),
            dma((SLOTS,)),
            dma((SLOTS,)),
            dma((YS,)),
            dma((YS,)),
            dma((YS,)),
            dma((YS,)),
        ],
        compiler_params=pltpu.CompilerParams(
            collective_id=0, has_side_effects=True, vmem_limit_bytes=40 << 20
        ),
    )(queries, keys, values, own_keys, own_values)


def solution(mesh):
    placed = (
        P("ctx", None),
        P(("ctx", "grp"), None),
        P(("ctx", "grp"), None),
        P("ctx", "grp"),
        P("ctx", "grp"),
    )
    return jax.shard_map(
        local, mesh=mesh, in_specs=placed, out_specs=P("ctx", "grp"), check_vma=False
    )
```

time: 1780 us -> 76.1 us (0.04)
  waiting for transfers between devices: 1240 us -> 0 us
  starting transfers between devices: 248 us -> 0 us
  blocking collectives: 152 us -> 0 us
  matrix products: 76.8 us -> 0 us
  Pallas kernels: 0 us -> 71.2 us
    ppermute x127 -> x0, waiting for transfers between devices: 1230 us -> none  [shifted(): return lax.ppermute(x, axis, [(i, (i + by) % count) for i in range(count)])]
    ppermute x127 -> x0, starting transfers between devices: 247 us -> none  [shifted(): return lax.ppermute(x, axis, [(i, (i + by) % count) for i in range(count)])]
    all_gather x2 -> x0, blocking collectives: 152 us -> none  [joined(): everything = jax.tree.map(lambda part: lax.all_gather(part, axis), x)]
    dot_general x256 -> x0, matrix products: 76.8 us -> none  [the longest x128 43.1 us: absorb(): jnp.einsum('gkr,kgh->grh', weights.astype(jnp.bfloat16), block_values, pr...]
    pallas_call x0 -> x1, Pallas kernels: none -> 71.2 us  [local(): pl.pallas_call(kernel, out_shape=jax.ShapeDtypeStruct((ROWS, GROUP * HS),...]
  transfers between devices with their start and end apart: 128 -> 0, of which waited for: 128 -> 0; matrix products, arithmetic and copies ran while one was open for 0% -> 0% of each run, Pallas kernels for 0% -> 0%
where the time goes in v1:
time: 76.1 us; the launch traced here: 75.8 us
  Pallas kernels  71.2 us (94%)
  local copies, waits for them, and re-layouts  4.6 us (6%)
    pallas_call x1, Pallas kernels, local(): pl.pallas_call(kernel, out_shape=jax.ShapeDtypeStruct((ROWS, GROUP * HS),...  71.2 us
    unnamed x11, local copies, waits for them, and re-layouts  4.6 us

profile of v1, /device:TPU:1, one launch (start us, length us, event | category | flops | bytes accessed | tf_op | source)
XLA Modules:
  0.0 75.8 jit_solution(5295396906277503863)
XLA Ops:
  0.0 0.0 copy-start
  0.0 0.9 %copy-done = bf16[16,6144]{1,0:T(8,128)(2,1)S(1)} copy-done((bf16[16,6144]{1,0:T(8,128)(2,1)S(1)}, bf16[16,6144]{1,0:T(8,128)(2,1)}, u32[]{:S(2)}) %copy-start) | copy-done | bytes 196632
  0.9 0.0 copy-start.1
  0.9 0.8 %copy-done.1 = bf16[60,512]{1,0:T(8,128)(2,1)S(1)} copy-done((bf16[60,512]{1,0:T(8,128)(2,1)S(1)}, bf16[60,512]{1,0:T(8,128)(2,1)}, u32[]{:S(2)}) %copy-start.1) | copy-done | bytes 61464
  1.8 0.0 copy-start.2
  1.8 0.8 %copy-done.2 = bf16[60,512]{1,0:T(8,128)(2,1)S(1)} copy-done((bf16[60,512]{1,0:T(8,128)(2,1)S(1)}, bf16[60,512]{1,0:T(8,128)(2,1)}, u32[]{:S(2)}) %copy-start.2) | copy-done | bytes 61464
  2.6 0.0 copy-start.3
  2.6 0.7 copy-done.3
  3.3 0.0 copy-start.4
  3.3 0.7 copy-done.4
  4.0 71.2 %shard_map.55 = bf16[16,1536]{1,0:T(8,128)(2,1)S(1)} custom-call(bf16[16,6144]{1,0:T(8,128)(2,1)S(1)} %copy-done, bf16[60,512]{1,0:T(8,128)(2,1)S(1)} %copy-done.1, bf16[60,512]{1,0:T(8,128)(2,1)S(1)} %copy-done.2, bf16[16,128]{1,0:T(8,128)(2,1)S(1)} %copy-done.3, bf16[16,128]{1,0:T(8,128)(2,1)S(1)} %copy-done.4), custom_call_target="tpu_custom_call" | custom-call | tf_op jit(solution)/shard_map/pallas_call | solution.py:327
  75.2 0.6 copy.7
Async XLA Ops:
  0.0 0.9 %copy-start = (bf16[16,6144]{1,0:T(8,128)(2,1)S(1)}, bf16[16,6144]{1,0:T(8,128)(2,1)}, u32[]{:S(2)}) copy-start(bf16[16,6144]{1,0:T(8,128)(2,1)} %q_ref.1) | copy-start | bytes 589828
  0.9 0.8 %copy-start.1 = (bf16[60,512]{1,0:T(8,128)(2,1)S(1)}, bf16[60,512]{1,0:T(8,128)(2,1)}, u32[]{:S(2)}) copy-start(bf16[60,512]{1,0:T(8,128)(2,1)} %k_ref.1) | copy-start | bytes 184324
  1.8 0.8 %copy-start.2 = (bf16[60,512]{1,0:T(8,128)(2,1)S(1)}, bf16[60,512]{1,0:T(8,128)(2,1)}, u32[]{:S(2)}) copy-start(bf16[60,512]{1,0:T(8,128)(2,1)} %v_ref.1) | copy-start | bytes 184324
  2.6 0.7 copy-start.3
  3.3 0.7 copy-start.4

commit v2 on v1

--- a/solution.py
+++ b/solution.py
@@ -36,10 +36,18 @@
 
 
 def kernel(
-    q_ref, k_ref, v_ref, ok_ref, ov_ref, out_ref,
-    pad32, kvst, qs, qbuf, kv, sib, acc, top, own, omsg, orecv,
+    q_hbm, k_hbm, v_hbm, ok_hbm, ov_hbm, out_ref,
+    q_ref, k_ref, v_ref, ok_ref, ov_ref, in_sem, pad32, kvst, qs, qbuf, kv, sib, acc, top, own, omsg, orecv,
     first_send, ring_send, ring_recv, sib_send, sib_recv, q_send, q_recv, o_send, o_recv,
 ):
+    fetches = [
+        pltpu.make_async_copy(source, to, in_sem.at[i])
+        for i, (source, to) in enumerate(
+            ((k_hbm, k_ref), (v_hbm, v_ref), (q_hbm, q_ref), (ok_hbm, ok_ref), (ov_hbm, ov_ref))
+        )
+    ]
+    for fetch in fetches:
+        fetch.start()
     ctx, grp = lax.axis_index("ctx"), lax.axis_index("grp")
     xhi, z, y = lax.rem(ctx, 2), lax.rem(ctx // 2, ZS), ctx // (2 * ZS)
     xlo, c = grp // 2, lax.rem(grp, 2)
@@ -83,6 +91,7 @@
         greet(device(q_from_x, y, z, q_from_c))
 
     for which, ref in ((0, k_ref), (1, v_ref)):
+        fetches[which].wait()
         rows = ref[...].astype(jnp.float32)
         pad32[0:KEYS, :] = rows
         if which == 0:
@@ -91,9 +100,6 @@
             pad32[KEYS:PAD, :] = jnp.zeros((PAD - KEYS, KVH * HS), jnp.float32)
         for h in range(KVH):
             kvst[h, which] = pad32[:, h * HS : (h + 1) * HS].astype(jnp.bfloat16)
-    for h in range(KVH * GROUP):
-        qs[h] = q_ref[:, h * HS : (h + 1) * HS]
-
     expected = 2 * XS + XS - 1 + 1 + 2 * YS - 1
     pl.semaphore_wait(barrier, jnp.where(q_self, expected, expected + 1))
 
@@ -124,6 +130,10 @@
             first(dz, dx).start()
     for dx in (2, 1, 3):
         first(2, dx).start()
+    kv[0, x] = kvst[mine]
+    fetches[2].wait()
+    for h in range(KVH * GROUP):
+        qs[h] = q_ref[:, h * HS : (h + 1) * HS]
     for dy in (2, 1, 3):
         query(dy).start()
 
@@ -134,8 +144,6 @@
     @pl.when(q_self)
     def _():
         qbuf[0] = qs[pl.ds(mine * GROUP, GROUP)]
-
-    kv[0, x] = kvst[mine]
 
     def forward(d, slot, to_slot, piece):
         return pltpu.make_async_remote_copy(
@@ -159,6 +167,9 @@
             device_id=sibling,
             device_id_type=MESH,
         )
+
+    fetches[3].wait()
+    fetches[4].wait()
 
     lane = lax.broadcasted_iota(jnp.int32, (ROWS, HS), 1)
     own_scores = jnp.zeros((ROWS, HS), jnp.float32)
@@ -166,7 +177,7 @@
     own_key = ok_ref[...].astype(jnp.float32)
     for h in range(GROUP):
         product = qs[group * GROUP + h].astype(jnp.float32) * own_key
-        score = jnp.sum(product, axis=1, keepdims=True) * SCALE
+        score = jnp.sum(product, axis=1, keepdims=True)
         own_scores = jnp.where(lane == h, score, own_scores)
     own[...] = own_scores
 
@@ -176,33 +187,36 @@
     ones = jnp.where(real, 1.0, 0.0).astype(jnp.bfloat16).reshape(8 * PAD, HS)
 
     def block_of(slot):
-        keys = jnp.concatenate(
-            [kv[slot, :, 0].reshape(4 * PAD, HS), sib[slot, :, 0].reshape(4 * PAD, HS)], axis=0
-        )
-        values = jnp.concatenate(
-            [kv[slot, :, 1].reshape(4 * PAD, HS), sib[slot, :, 1].reshape(4 * PAD, HS)], axis=0
-        )
-        return keys, jnp.concatenate([values, ones], axis=1)
+        keys = [held[slot, :, 0].reshape(4 * PAD, HS) for held in (kv, sib)]
+        values = [held[slot, :, 1].reshape(4 * PAD, HS) for held in (kv, sib)]
+        values = jnp.concatenate(values, axis=0)
+        return jnp.concatenate(keys, axis=0), jnp.concatenate([values, ones], axis=1)
 
     def absorb(i, keys, values):
-        scores = nt(qbuf[i].reshape(QB, HS), keys) * SCALE
-        before = top[i][:, :1]
+        scores = nt(qbuf[i].reshape(QB, HS), keys)
+        before = top[i]
         best = jnp.max(scores, axis=1, keepdims=True).astype(jnp.bfloat16).astype(jnp.float32)
-        now = jnp.maximum(before, best)
-        weights = jnp.exp2(scores - now).astype(jnp.bfloat16)
-        mixed = jnp.dot(weights, values, preferred_element_type=jnp.float32)
-        acc[i] = acc[i] * jnp.exp2(before - now) + mixed
-        top[i] = jnp.broadcast_to(now, (QB, HS))
-
-    def compute(slot):
-        across(slot).wait_recv()
-        keys, values = block_of(slot)
-
-        def turn(i, _):
+        now = jnp.maximum(before, jnp.broadcast_to(best, (QB, HS)))
+        top[i] = now
+        scaled = now * SCALE
+        weights = [
+            jnp.exp2(scores[:, k : k + HS] * SCALE - scaled).astype(jnp.bfloat16)
+            for k in range(0, keys.shape[0], HS)
+        ]
+        mixed = jnp.dot(
+            jnp.concatenate(weights, axis=1), values, preferred_element_type=jnp.float32
+        )
+        factor = jnp.exp2((before - now) * SCALE)
+        acc[i] = acc[i] * jnp.concatenate([factor, factor], axis=1) + mixed
+
+    def compute(*slots):
+        for slot in slots:
+            across(slot).wait_recv()
+        blocks = [block_of(slot) for slot in slots]
+        keys = jnp.concatenate([block[0] for block in blocks], axis=0)
+        values = jnp.concatenate([block[1] for block in blocks], axis=0)
+        for i in range(YS):
             absorb(i, keys, values)
-            return 0
-
-        lax.fori_loop(0, YS, turn, 0)
 
     for dx in (1, 2, 3):
         arrived(0, 0, at_x(dx))
@@ -214,33 +228,33 @@
     def _():
         query(0).wait_recv()
 
-    def step(s, _):
+    def pass_on(s):
         slot = 2 * s - 1
         for piece in range(XS):
             for d in (0, 1):
                 arrived(d, slot + d, piece)
-                forward(d, slot + d, slot + 2 + d, piece).start()
+                to_slot = jnp.minimum(slot + 2 + d, SLOTS - 1)
+
+                @pl.when(jnp.logical_or(s < HALF - 1, piece // 2 == d))
+                def _():
+                    forward(d, slot + d, to_slot, piece).start()
+
         for d in (0, 1):
             across(slot + d).start()
-        compute(slot - 1)
-        compute(slot)
+
+    pass_on(jnp.int32(1))
+    compute(0)
+
+    def step(s, _):
+        pass_on(s)
+        compute(2 * s - 3, 2 * s - 2)
         return 0
 
-    lax.fori_loop(1, HALF - 1, step, 0)
-    slot = 2 * HALF - 3
-    for piece in range(XS):
-        for d in (0, 1):
-            arrived(d, slot + d, piece)
-            if piece // 2 == d:
-                forward(d, slot + d, SLOTS - 1, piece).start()
-    for d in (0, 1):
-        across(slot + d).start()
-    compute(slot - 1)
-    compute(slot)
+    lax.fori_loop(2, HALF, step, 0)
+    compute(SLOTS - 3, SLOTS - 2)
     for piece in range(XS):
         arrived(piece // 2, SLOTS - 1, piece)
     across(SLOTS - 1).start()
-    compute(SLOTS - 2)
 
     def result(dy):
         return pltpu.make_async_remote_copy(
@@ -268,6 +282,32 @@
         omsg[dy, GROUP] = stats.astype(jnp.bfloat16)
         result(dy).start()
 
+    for dz in range(3):
+        for dx in range(XS):
+            if dz < 2 or dx:
+                first(dz, dx).wait_send()
+    for dy in (1, 2, 3):
+        query(dy).wait_send()
+
+    @pl.when(jnp.logical_not(q_self))
+    def _():
+        query(0).wait_send()
+
+    def sent(slot, _):
+        for piece in range(XS):
+            forward(0, slot, slot, piece).wait_send()
+        return 0
+
+    lax.fori_loop(1, SLOTS - 3, sent, 0)
+    for piece in range(XS):
+        forward(0, SLOTS - 3 + piece // 2, SLOTS - 1, piece).wait_send()
+
+    def crossed(slot, _):
+        across(slot).wait_send()
+        return 0
+
+    lax.fori_loop(0, SLOTS, crossed, 0)
+
     for dy in range(YS):
         result(dy).wait_recv()
     largest = own[...]
@@ -277,8 +317,8 @@
         tops.append(stats)
         totals.append(pltpu.roll(stats, HS - LANES, 1) + pltpu.roll(stats, HS - 2 * LANES, 1))
         largest = jnp.maximum(largest, stats)
-    own_factor = jnp.exp2(own[...] - largest)
-    factors = [jnp.exp2(t - largest) for t in tops]
+    own_factor = jnp.exp2((own[...] - largest) * SCALE)
+    factors = [jnp.exp2((t - largest) * SCALE) for t in tops]
     total = own_factor
     for factor, part in zip(factors, totals):
         total = total + factor * part
@@ -290,32 +330,6 @@
         for i in range(YS):
             mixed = mixed + factors[i][:, h : h + 1] * orecv[i, h].astype(jnp.float32)
         out_ref[:, h * HS : (h + 1) * HS] = mixed.astype(jnp.bfloat16)
-
-    for dz in range(3):
-        for dx in range(XS):
-            if dz < 2 or dx:
-                first(dz, dx).wait_send()
-    for dy in (1, 2, 3):
-        query(dy).wait_send()
-
-    @pl.when(jnp.logical_not(q_self))
-    def _():
-        query(0).wait_send()
-
-    def sent(slot, _):
-        for piece in range(XS):
-            forward(0, slot, slot, piece).wait_send()
-        return 0
-
-    lax.fori_loop(1, SLOTS - 3, sent, 0)
-    for piece in range(XS):
-        forward(0, slot + piece // 2, SLOTS - 1, piece).wait_send()
-
-    def crossed(slot, _):
-        across(slot).wait_send()
-        return 0
-
-    lax.fori_loop(0, SLOTS, crossed, 0)
     for dy in range(YS):
         result(dy).wait_send()
 
@@ -327,9 +341,15 @@
     return pl.pallas_call(
         kernel,
         out_shape=jax.ShapeDtypeStruct((ROWS, GROUP * HS), bf16),
-        in_specs=[vmem] * 5,
+        in_specs=[pl.BlockSpec(memory_space=pl.ANY)] * 5,
         out_specs=vmem,
         scratch_shapes=[
+            pltpu.VMEM((ROWS, KVH * GROUP * HS), bf16),
+            pltpu.VMEM((KEYS, KVH * HS), bf16),
+            pltpu.VMEM((KEYS, KVH * HS), bf16),
+            pltpu.VMEM((ROWS, HS), bf16),
+            pltpu.VMEM((ROWS, HS), bf16),
+            dma((5,)),
             pltpu.VMEM((PAD, KVH * HS), f32),
             pltpu.VMEM((KVH, 2, PAD, HS), bf16),
             pltpu.VMEM((KVH * GROUP, ROWS, HS), bf16),
@@ -352,7 +372,7 @@
             dma((YS,)),
         ],
         compiler_params=pltpu.CompilerParams(
-            collective_id=0, has_side_effects=True, vmem_limit_bytes=40 << 20
+            collective_id=0, has_side_effects=True, vmem_limit_bytes=60 << 20
         ),
     )(queries, keys, values, own_keys, own_values)
 

time: 76.1 us -> 60.8 us (0.80)
  Pallas kernels: 71.2 us -> 59.2 us
  local copies, waits for them, and re-layouts: 4.6 us -> 1.42 us
    pallas_call x1, Pallas kernels: 71.2 us -> 59.2 us  [local(): pl.pallas_call(kernel, out_shape=jax.ShapeDtypeStruct((ROWS, GROUP * HS),...]
    unnamed x11 -> x1, local copies, waits for them, and re-layouts: 4.6 us -> 1.42 us
where the time goes in v2:
time: 60.8 us; the launch traced here: 60.6 us
  Pallas kernels  59.2 us (97%)
  local copies, waits for them, and re-layouts  1.42 us (2%)
    pallas_call x1, Pallas kernels, local(): pl.pallas_call(kernel, out_shape=jax.ShapeDtypeStruct((ROWS, GROUP * HS),...  59.2 us
    unnamed x1, local copies, waits for them, and re-layouts  1.42 us

profile of v2, /device:TPU:1, one launch (start us, length us, event | category | flops | bytes accessed | tf_op | source)
XLA Modules:
  0.0 60.6 jit_solution(10442539720040326690)
XLA Ops:
  0.0 59.2 %shard_map.55 = bf16[16,1536]{1,0:T(8,128)(2,1)} custom-call(bf16[16,6144]{1,0:T(8,128)(2,1)} %q_hbm.1, bf16[60,512]{1,0:T(8,128)(2,1)} %k_hbm.1, bf16[60,512]{1,0:T(8,128)(2,1)} %v_hbm.1, bf16[16,128]{1,0:T(8,128)(2,1)} %ok_hbm.1, bf16[16,128]{1,0:T(8,128)(2,1)} %ov_hbm.1), custom_call_target="tpu_custom_call" | custom-call | tf_op jit(solution)/shard_map/pallas_call | solution.py:341
  59.2 1.4 %copy.7 = bf16[16,1536]{1,0:T(8,128)(2,1)} copy(bf16[16,1536]{1,0:T(8,128)(2,1)} %shard_map.55) | data formatting | bytes 98304

commit v3 on v2

--- a/solution.py
+++ b/solution.py
@@ -62,13 +62,9 @@
 
     z_next = (lax.rem(z + 1, ZS), lax.rem(z + ZS - 1, ZS), z)
     sibling = device(x, y, z, 1 - c)
-    q_x = jnp.where(c == 0, x, XS - 1 - x)
-    q_self = jnp.logical_and(c == 0, xhi == 0)
-    q_from_own = c == xhi
-    q_from_x = jnp.where(q_from_own, x, XS - 1 - x)
-    q_from_c = jnp.where(q_from_own, 0, 1)
+    q_self = c == xhi
+    q_x = jnp.where(q_self, x, XS - 1 - x)
     o_x, o_c = 2 * c + mine // 2, lax.rem(mine, 2)
-    o_from_x, o_from_c = 2 * c + 1 - xlo, xhi
 
     barrier = pltpu.get_barrier_semaphore()
 
@@ -76,19 +72,17 @@
         pl.semaphore_signal(barrier, inc=1, device_id=to, device_id_type=MESH)
 
     for dz in (0, 1):
-        for dx in range(XS):
+        for dx in (1, 3, 0):
             greet(device(at_x(dx), y, z_next[dz], c))
     for dx in range(1, XS):
         greet(device(at_x(dx), y, z, c))
     greet(sibling)
-    for dy in range(YS):
-        greet(device(o_from_x, at_y(dy), z, o_from_c))
-        if dy:
-            greet(device(q_from_x, at_y(dy), z, q_from_c))
+    for dy in range(1, YS):
+        greet(device(q_x, at_y(dy), z, xhi))
 
     @pl.when(jnp.logical_not(q_self))
     def _():
-        greet(device(q_from_x, y, z, q_from_c))
+        greet(device(q_x, y, z, xhi))
 
     for which, ref in ((0, k_ref), (1, v_ref)):
         fetches[which].wait()
@@ -100,7 +94,7 @@
             pad32[KEYS:PAD, :] = jnp.zeros((PAD - KEYS, KVH * HS), jnp.float32)
         for h in range(KVH):
             kvst[h, which] = pad32[:, h * HS : (h + 1) * HS].astype(jnp.bfloat16)
-    expected = 2 * XS + XS - 1 + 1 + 2 * YS - 1
+    expected = 2 * (XS - 1) + XS - 1 + 1 + YS - 1
     pl.semaphore_wait(barrier, jnp.where(q_self, expected, expected + 1))
 
     def first(dz, dx):
@@ -125,10 +119,11 @@
             device_id_type=MESH,
         )
 
-    for dx in (2, 1, 3, 0):
+    first(2, 2).start()
+    for dx in (1, 3, 0):
         for dz in (0, 1):
             first(dz, dx).start()
-    for dx in (2, 1, 3):
+    for dx in (1, 3):
         first(2, dx).start()
     kv[0, x] = kvst[mine]
     fetches[2].wait()
@@ -218,7 +213,20 @@
         for i in range(YS):
             absorb(i, keys, values)
 
-    for dx in (1, 2, 3):
+    def relay(d):
+        return pltpu.make_async_remote_copy(
+            src_ref=kv.at[0, at_x(2)],
+            dst_ref=kv.at[1 + d, at_x(2)],
+            send_sem=first_send.at[d, 2],
+            recv_sem=ring_recv.at[1 + d, at_x(2)],
+            device_id=device(x, y, z_next[d], c),
+            device_id_type=MESH,
+        )
+
+    arrived(0, 0, at_x(2))
+    for d in (0, 1):
+        relay(d).start()
+    for dx in (1, 3):
         arrived(0, 0, at_x(dx))
     across(0).start()
     for dy in (1, 2, 3):
@@ -228,14 +236,16 @@
     def _():
         query(0).wait_recv()
 
+    pieces = [(at_x(0), 0), (at_x(1), 0), (at_x(3), 1), (at_x(2), 1)]
+
     def pass_on(s):
         slot = 2 * s - 1
-        for piece in range(XS):
+        for piece, side in pieces:
             for d in (0, 1):
                 arrived(d, slot + d, piece)
                 to_slot = jnp.minimum(slot + 2 + d, SLOTS - 1)
 
-                @pl.when(jnp.logical_or(s < HALF - 1, piece // 2 == d))
+                @pl.when(jnp.logical_or(s < HALF - 1, side == d))
                 def _():
                     forward(d, slot + d, to_slot, piece).start()
 
@@ -252,8 +262,8 @@
 
     lax.fori_loop(2, HALF, step, 0)
     compute(SLOTS - 3, SLOTS - 2)
-    for piece in range(XS):
-        arrived(piece // 2, SLOTS - 1, piece)
+    for piece, side in pieces:
+        arrived(side, SLOTS - 1, piece)
     across(SLOTS - 1).start()
 
     def result(dy):
@@ -299,8 +309,8 @@
         return 0
 
     lax.fori_loop(1, SLOTS - 3, sent, 0)
-    for piece in range(XS):
-        forward(0, SLOTS - 3 + piece // 2, SLOTS - 1, piece).wait_send()
+    for piece, side in pieces:
+        forward(0, SLOTS - 3 + side, SLOTS - 1, piece).wait_send()
 
     def crossed(slot, _):
         across(slot).wait_send()

time: 60.8 us -> 59.4 us (0.977)
  Pallas kernels: 59.2 us -> 57.8 us
    pallas_call x1, Pallas kernels: 59.2 us -> 57.8 us  [local(): pl.pallas_call(kernel, out_shape=jax.ShapeDtypeStruct((ROWS, GROUP * HS),...]
where the time goes in v3:
time: 59.4 us; the launch traced here: 59.2 us
  Pallas kernels  57.8 us (97%)
  local copies, waits for them, and re-layouts  1.42 us (2%)
    pallas_call x1, Pallas kernels, local(): pl.pallas_call(kernel, out_shape=jax.ShapeDtypeStruct((ROWS, GROUP * HS),...  57.8 us
    unnamed x1, local copies, waits for them, and re-layouts  1.42 us

profile of v3, /device:TPU:1, one launch (start us, length us, event | category | flops | bytes accessed | tf_op | source)
XLA Modules:
  0.0 59.2 jit_solution(8785429129276225113)
XLA Ops:
  0.0 57.8 %shard_map.55 = bf16[16,1536]{1,0:T(8,128)(2,1)} custom-call(bf16[16,6144]{1,0:T(8,128)(2,1)} %q_hbm.1, bf16[60,512]{1,0:T(8,128)(2,1)} %k_hbm.1, bf16[60,512]{1,0:T(8,128)(2,1)} %v_hbm.1, bf16[16,128]{1,0:T(8,128)(2,1)} %ok_hbm.1, bf16[16,128]{1,0:T(8,128)(2,1)} %ov_hbm.1), custom_call_target="tpu_custom_call" | custom-call | tf_op jit(solution)/shard_map/pallas_call | solution.py:351
  57.8 1.4 %copy.7 = bf16[16,1536]{1,0:T(8,128)(2,1)} copy(bf16[16,1536]{1,0:T(8,128)(2,1)} %shard_map.55) | data formatting | bytes 98304

commit v4 on v3

--- a/solution.py
+++ b/solution.py
@@ -17,7 +17,8 @@
 KEYS = 60
 PAD = 64
 HALF = ZS // 2
-SLOTS = ZS
+PIECES = 2 * XS
+PLACE = (0, 1, 3, 2)
 SCALE = math.log2(math.e) / math.sqrt(HS)
 QB = GROUP * ROWS
 LANES = 16
@@ -37,8 +38,9 @@
 
 def kernel(
     q_hbm, k_hbm, v_hbm, ok_hbm, ov_hbm, out_ref,
-    q_ref, k_ref, v_ref, ok_ref, ov_ref, in_sem, pad32, kvst, qs, qbuf, kv, sib, acc, top, own, omsg, orecv,
-    first_send, ring_send, ring_recv, sib_send, sib_recv, q_send, q_recv, o_send, o_recv,
+    q_ref, k_ref, v_ref, ok_ref, ov_ref, in_sem, pad32, kvst, qs, qbuf, near, kv, sib, far, acc, top, own, omsg, orecv,
+    first_send, relay_send, ring_send, ring_recv, last_send, last_recv, sib_send, sib_recv,
+    near_recv, q_send, q_recv, o_send, o_recv,
 ):
     fetches = [
         pltpu.make_async_copy(source, to, in_sem.at[i])
@@ -60,7 +62,9 @@
     def at_y(dy):
         return lax.rem(y + dy, YS)
 
-    z_next = (lax.rem(z + 1, ZS), lax.rem(z + ZS - 1, ZS), z)
+    z_up, z_down = lax.rem(z + 1, ZS), lax.rem(z + ZS - 1, ZS)
+    z_to = jnp.where(c == 0, z_up, z_down)
+    z_from = jnp.where(c == 0, z_down, z_up)
     sibling = device(x, y, z, 1 - c)
     q_self = c == xhi
     q_x = jnp.where(q_self, x, XS - 1 - x)
@@ -71,9 +75,10 @@
     def greet(to):
         pl.semaphore_signal(barrier, inc=1, device_id=to, device_id_type=MESH)
 
-    for dz in (0, 1):
-        for dx in (1, 3, 0):
-            greet(device(at_x(dx), y, z_next[dz], c))
+    for dx in (1, 3, 0):
+        for core in (0, 1):
+            greet(device(at_x(dx), y, z_from, core))
+    greet(device(x, y, z_to, 1 - c))
     for dx in range(1, XS):
         greet(device(at_x(dx), y, z, c))
     greet(sibling)
@@ -94,18 +99,28 @@
             pad32[KEYS:PAD, :] = jnp.zeros((PAD - KEYS, KVH * HS), jnp.float32)
         for h in range(KVH):
             kvst[h, which] = pad32[:, h * HS : (h + 1) * HS].astype(jnp.bfloat16)
-    expected = 2 * (XS - 1) + XS - 1 + 1 + YS - 1
+    expected = 2 * (XS - 1) + 1 + XS - 1 + 1 + YS - 1
     pl.semaphore_wait(barrier, jnp.where(q_self, expected, expected + 1))
 
-    def first(dz, dx):
+    def here(dx):
         to = at_x(dx)
-        slot = (1, 2, 0)[dz]
         return pltpu.make_async_remote_copy(
             src_ref=kvst.at[head_of(to)],
-            dst_ref=kv.at[slot, x],
-            send_sem=first_send.at[dz, dx],
-            recv_sem=ring_recv.at[slot, x],
-            device_id=device(to, y, z_next[dz], c),
+            dst_ref=near.at[PLACE[(XS - dx) % XS]],
+            send_sem=first_send.at[2, dx],
+            recv_sem=near_recv.at[PLACE[(XS - dx) % XS]],
+            device_id=device(to, y, z, c),
+            device_id_type=MESH,
+        )
+
+    def first(way, dx):
+        to = at_x(dx)
+        return pltpu.make_async_remote_copy(
+            src_ref=kvst.at[head_of(to)],
+            dst_ref=kv.at[0, 2 * PLACE[(XS - dx) % XS] + c],
+            send_sem=first_send.at[way, dx],
+            recv_sem=ring_recv.at[0, 2 * PLACE[(XS - dx) % XS] + c],
+            device_id=device(to, y, (z_up, z_down)[way], way),
             device_id_type=MESH,
         )
 
@@ -119,13 +134,13 @@
             device_id_type=MESH,
         )
 
-    first(2, 2).start()
+    here(2).start()
     for dx in (1, 3, 0):
-        for dz in (0, 1):
-            first(dz, dx).start()
+        for way in (0, 1):
+            first(way, dx).start()
     for dx in (1, 3):
-        first(2, dx).start()
-    kv[0, x] = kvst[mine]
+        here(dx).start()
+    near[0] = kvst[mine]
     fetches[2].wait()
     for h in range(KVH * GROUP):
         qs[h] = q_ref[:, h * HS : (h + 1) * HS]
@@ -140,26 +155,44 @@
     def _():
         qbuf[0] = qs[pl.ds(mine * GROUP, GROUP)]
 
-    def forward(d, slot, to_slot, piece):
-        return pltpu.make_async_remote_copy(
-            src_ref=kv.at[slot, piece],
-            dst_ref=kv.at[to_slot, piece],
-            send_sem=ring_send.at[slot, piece],
-            recv_sem=ring_recv.at[to_slot, piece],
-            device_id=device(x, y, z_next[d], c),
-            device_id_type=MESH,
-        )
-
-    def arrived(d, slot, piece):
-        forward(d, slot, slot, piece).wait_recv()
-
-    def across(slot):
-        return pltpu.make_async_remote_copy(
-            src_ref=kv.at[slot],
-            dst_ref=sib.at[slot],
-            send_sem=sib_send.at[slot],
-            recv_sem=sib_recv.at[slot],
+    def forward(step, piece):
+        return pltpu.make_async_remote_copy(
+            src_ref=kv.at[step, piece],
+            dst_ref=kv.at[step + 1, piece],
+            send_sem=ring_send.at[step, piece],
+            recv_sem=ring_recv.at[step + 1, piece],
+            device_id=device(x, y, z_to, c),
+            device_id_type=MESH,
+        )
+
+    def arrived(step, piece):
+        pltpu.make_async_remote_copy(
+            src_ref=kv.at[step, piece],
+            dst_ref=kv.at[step, piece],
+            send_sem=ring_send.at[step, piece],
+            recv_sem=ring_recv.at[step, piece],
+            device_id=device(x, y, z_to, c),
+            device_id_type=MESH,
+        ).wait_recv()
+
+    def across(step, part):
+        rows = pl.ds(part * XS, XS)
+        return pltpu.make_async_remote_copy(
+            src_ref=kv.at[step, rows],
+            dst_ref=sib.at[step, rows],
+            send_sem=sib_send.at[step, part],
+            recv_sem=sib_recv.at[step, part],
             device_id=sibling,
+            device_id_type=MESH,
+        )
+
+    def last(piece, i, core):
+        return pltpu.make_async_remote_copy(
+            src_ref=kv.at[HALF - 2, piece],
+            dst_ref=far.at[piece],
+            send_sem=last_send.at[core, i],
+            recv_sem=last_recv.at[piece],
+            device_id=device(x, y, z_to, c if core == 0 else 1 - c),
             device_id_type=MESH,
         )
 
@@ -178,14 +211,12 @@
 
     top[...] = jnp.full(top.shape, -1e30, jnp.float32)
     acc[...] = jnp.zeros(acc.shape, jnp.float32)
-    real = lax.broadcasted_iota(jnp.int32, (8, PAD, HS), 1) < KEYS
-    ones = jnp.where(real, 1.0, 0.0).astype(jnp.bfloat16).reshape(8 * PAD, HS)
-
-    def block_of(slot):
-        keys = [held[slot, :, 0].reshape(4 * PAD, HS) for held in (kv, sib)]
-        values = [held[slot, :, 1].reshape(4 * PAD, HS) for held in (kv, sib)]
-        values = jnp.concatenate(values, axis=0)
-        return jnp.concatenate(keys, axis=0), jnp.concatenate([values, ones], axis=1)
+    real = lax.broadcasted_iota(jnp.int32, (PIECES, PAD, HS), 1) < KEYS
+    ones = jnp.where(real, 1.0, 0.0).astype(jnp.bfloat16).reshape(PIECES * PAD, HS)
+
+    def block_of(held):
+        values = held[:, 1].reshape(PIECES * PAD, HS)
+        return held[:, 0].reshape(PIECES * PAD, HS), jnp.concatenate([values, ones], axis=1)
 
     def absorb(i, keys, values):
         scores = nt(qbuf[i].reshape(QB, HS), keys)
@@ -204,31 +235,69 @@
         factor = jnp.exp2((before - now) * SCALE)
         acc[i] = acc[i] * jnp.concatenate([factor, factor], axis=1) + mixed
 
-    def compute(*slots):
-        for slot in slots:
-            across(slot).wait_recv()
-        blocks = [block_of(slot) for slot in slots]
+    def compute(*blocks):
+        blocks = [block_of(block) for block in blocks]
         keys = jnp.concatenate([block[0] for block in blocks], axis=0)
         values = jnp.concatenate([block[1] for block in blocks], axis=0)
         for i in range(YS):
             absorb(i, keys, values)
 
-    def relay(d):
-        return pltpu.make_async_remote_copy(
-            src_ref=kv.at[0, at_x(2)],
-            dst_ref=kv.at[1 + d, at_x(2)],
-            send_sem=first_send.at[d, 2],
-            recv_sem=ring_recv.at[1 + d, at_x(2)],
-            device_id=device(x, y, z_next[d], c),
-            device_id_type=MESH,
-        )
-
-    arrived(0, 0, at_x(2))
-    for d in (0, 1):
-        relay(d).start()
-    for dx in (1, 3):
-        arrived(0, 0, at_x(dx))
-    across(0).start()
+    def relay(way):
+        return pltpu.make_async_remote_copy(
+            src_ref=near.at[PLACE[2]],
+            dst_ref=kv.at[0, 2 * PLACE[2] + c],
+            send_sem=relay_send.at[way],
+            recv_sem=ring_recv.at[0, 2 * PLACE[2] + c],
+            device_id=device(x, y, (z_up, z_down)[way], way),
+            device_id_type=MESH,
+        )
+
+    def near_across():
+        return pltpu.make_async_remote_copy(
+            src_ref=near.at[pl.ds(0, XS)],
+            dst_ref=near.at[pl.ds(XS, XS)],
+            send_sem=sib_send.at[HALF - 1, 0],
+            recv_sem=sib_recv.at[HALF - 1, 0],
+            device_id=sibling,
+            device_id_type=MESH,
+        )
+
+    def came(dx):
+        here(dx).wait_recv()
+
+    came(2)
+    for way in (0, 1):
+        relay(way).start()
+    came(1)
+    came(3)
+    near_across().start()
+    def pass_on(step, send):
+        for piece in range(PIECES):
+            arrived(step, piece)
+            send(step, piece)
+            if piece % XS == XS - 1:
+                across(step, piece // XS).start()
+
+    def to_next(step, piece):
+        forward(step, piece).start()
+
+    def to_both(step, piece):
+        @pl.when(c == piece // XS)
+        def _():
+            for core in (0, 1):
+                last(piece, piece % XS, core).start()
+
+    def crossed(step):
+        for part in (0, 1):
+            across(step, part).wait_recv()
+
+    def turn(step, _):
+        pass_on(step, to_next)
+        crossed(step - 1)
+        compute(sib.at[step - 1], kv.at[step])
+        return 0
+
+    pass_on(0, to_next)
     for dy in (1, 2, 3):
         query(dy).wait_recv()
 
@@ -236,35 +305,23 @@
     def _():
         query(0).wait_recv()
 
-    pieces = [(at_x(0), 0), (at_x(1), 0), (at_x(3), 1), (at_x(2), 1)]
-
-    def pass_on(s):
-        slot = 2 * s - 1
-        for piece, side in pieces:
-            for d in (0, 1):
-                arrived(d, slot + d, piece)
-                to_slot = jnp.minimum(slot + 2 + d, SLOTS - 1)
-
-                @pl.when(jnp.logical_or(s < HALF - 1, side == d))
-                def _():
-                    forward(d, slot + d, to_slot, piece).start()
-
-        for d in (0, 1):
-            across(slot + d).start()
-
-    pass_on(jnp.int32(1))
-    compute(0)
-
-    def step(s, _):
-        pass_on(s)
-        compute(2 * s - 3, 2 * s - 2)
-        return 0
-
-    lax.fori_loop(2, HALF, step, 0)
-    compute(SLOTS - 3, SLOTS - 2)
-    for piece, side in pieces:
-        arrived(side, SLOTS - 1, piece)
-    across(SLOTS - 1).start()
+    near_across().wait_recv()
+    compute(near, kv.at[0])
+    lax.fori_loop(1, HALF - 2, turn, 0)
+    pass_on(HALF - 2, to_both)
+    crossed(HALF - 3)
+    compute(sib.at[HALF - 3], kv.at[HALF - 2])
+    crossed(HALF - 2)
+    compute(sib.at[HALF - 2])
+    for piece in range(PIECES):
+        pltpu.make_async_remote_copy(
+            src_ref=far.at[piece],
+            dst_ref=far.at[piece],
+            send_sem=last_send.at[0, 0],
+            recv_sem=last_recv.at[piece],
+            device_id=sibling,
+            device_id_type=MESH,
+        ).wait_recv()
 
     def result(dy):
         return pltpu.make_async_remote_copy(
@@ -276,8 +333,7 @@
             device_id_type=MESH,
         )
 
-    across(SLOTS - 1).wait_recv()
-    keys, values = block_of(SLOTS - 1)
+    keys, values = block_of(far)
     for dy in (2, 1, 3, 0):
         absorb(dy, keys, values)
         omsg[dy, 0:GROUP] = acc[dy, :, :HS].astype(jnp.bfloat16).reshape(GROUP, ROWS, HS)
@@ -292,10 +348,12 @@
         omsg[dy, GROUP] = stats.astype(jnp.bfloat16)
         result(dy).start()
 
-    for dz in range(3):
-        for dx in range(XS):
-            if dz < 2 or dx:
-                first(dz, dx).wait_send()
+    for dx in (1, 2, 3):
+        here(dx).wait_send()
+    for way in (0, 1):
+        relay(way).wait_send()
+        for dx in (1, 3, 0):
+            first(way, dx).wait_send()
     for dy in (1, 2, 3):
         query(dy).wait_send()
 
@@ -303,20 +361,23 @@
     def _():
         query(0).wait_send()
 
-    def sent(slot, _):
-        for piece in range(XS):
-            forward(0, slot, slot, piece).wait_send()
+    def sent(step, _):
+        for piece in range(PIECES):
+            forward(step, piece).wait_send()
         return 0
 
-    lax.fori_loop(1, SLOTS - 3, sent, 0)
-    for piece, side in pieces:
-        forward(0, SLOTS - 3 + side, SLOTS - 1, piece).wait_send()
-
-    def crossed(slot, _):
-        across(slot).wait_send()
+    lax.fori_loop(0, HALF - 2, sent, 0)
+    for i in range(XS):
+        for core in (0, 1):
+            last(i, i, core).wait_send()
+    near_across().wait_send()
+
+    def across_sent(step, _):
+        for part in (0, 1):
+            across(step, part).wait_send()
         return 0
 
-    lax.fori_loop(0, SLOTS, crossed, 0)
+    lax.fori_loop(0, HALF - 1, across_sent, 0)
 
     for dy in range(YS):
         result(dy).wait_recv()
@@ -364,18 +425,24 @@
             pltpu.VMEM((KVH, 2, PAD, HS), bf16),
             pltpu.VMEM((KVH * GROUP, ROWS, HS), bf16),
             pltpu.VMEM((YS, GROUP, ROWS, HS), bf16),
-            pltpu.VMEM((SLOTS, XS, 2, PAD, HS), bf16),
-            pltpu.VMEM((SLOTS, XS, 2, PAD, HS), bf16),
+            pltpu.VMEM((PIECES, 2, PAD, HS), bf16),
+            pltpu.VMEM((HALF - 1, PIECES, 2, PAD, HS), bf16),
+            pltpu.VMEM((HALF - 1, PIECES, 2, PAD, HS), bf16),
+            pltpu.VMEM((PIECES, 2, PAD, HS), bf16),
             pltpu.VMEM((YS, QB, 2 * HS), f32),
             pltpu.VMEM((YS, QB, HS), f32),
             pltpu.VMEM((ROWS, HS), f32),
             pltpu.VMEM((YS, GROUP + 1, ROWS, HS), bf16),
             pltpu.VMEM((YS, GROUP + 1, ROWS, HS), bf16),
             dma((3, XS)),
-            dma((SLOTS, XS)),
-            dma((SLOTS, XS)),
-            dma((SLOTS,)),
-            dma((SLOTS,)),
+            dma((2,)),
+            dma((HALF - 1, PIECES)),
+            dma((HALF - 1, PIECES)),
+            dma((2, XS)),
+            dma((PIECES,)),
+            dma((HALF, 2)),
+            dma((HALF, 2)),
+            dma((XS,)),
             dma((YS,)),
             dma((YS,)),
             dma((YS,)),

time: 59.4 us -> 57.8 us (0.973)
  Pallas kernels: 57.8 us -> 56.2 us
    pallas_call x1, Pallas kernels: 57.8 us -> 56.2 us  [local(): pl.pallas_call(kernel, out_shape=jax.ShapeDtypeStruct((ROWS, GROUP * HS),...]
where the time goes in v4:
time: 57.8 us; the launch traced here: 57.6 us
  Pallas kernels  56.2 us (97%)
  local copies, waits for them, and re-layouts  1.42 us (2%)
    pallas_call x1, Pallas kernels, local(): pl.pallas_call(kernel, out_shape=jax.ShapeDtypeStruct((ROWS, GROUP * HS),...  56.2 us
    unnamed x1, local copies, waits for them, and re-layouts  1.42 us

profile of v4, /device:TPU:1, one launch (start us, length us, event | category | flops | bytes accessed | tf_op | source)
XLA Modules:
  0.0 57.6 jit_solution(10627243893536077280)
XLA Ops:
  0.0 56.2 %shard_map.55 = bf16[16,1536]{1,0:T(8,128)(2,1)} custom-call(bf16[16,6144]{1,0:T(8,128)(2,1)} %q_hbm.1, bf16[60,512]{1,0:T(8,128)(2,1)} %k_hbm.1, bf16[60,512]{1,0:T(8,128)(2,1)} %v_hbm.1, bf16[16,128]{1,0:T(8,128)(2,1)} %ok_hbm.1, bf16[16,128]{1,0:T(8,128)(2,1)} %ov_hbm.1), custom_call_target="tpu_custom_call" | custom-call | tf_op jit(solution)/shard_map/pallas_call | solution.py:412
  56.2 1.4 %copy.7 = bf16[16,1536]{1,0:T(8,128)(2,1)} copy(bf16[16,1536]{1,0:T(8,128)(2,1)} %shard_map.55) | data formatting | bytes 98304

commit v5 on v4

--- a/solution.py
+++ b/solution.py
@@ -135,8 +135,10 @@
         )
 
     here(2).start()
-    for dx in (1, 3, 0):
-        for way in (0, 1):
+    for way in (0, 1):
+        first(way, 0).start()
+    for way in (0, 1):
+        for dx in (1, 3):
             first(way, dx).start()
     for dx in (1, 3):
         here(dx).start()
@@ -235,11 +237,11 @@
         factor = jnp.exp2((before - now) * SCALE)
         acc[i] = acc[i] * jnp.concatenate([factor, factor], axis=1) + mixed
 
-    def compute(*blocks):
+    def compute(parts, *blocks):
         blocks = [block_of(block) for block in blocks]
         keys = jnp.concatenate([block[0] for block in blocks], axis=0)
         values = jnp.concatenate([block[1] for block in blocks], axis=0)
-        for i in range(YS):
+        for i in parts:
             absorb(i, keys, values)
 
     def relay(way):
@@ -271,12 +273,16 @@
     came(1)
     came(3)
     near_across().start()
-    def pass_on(step, send):
+    work_after = {1: (0,), 3: (1,), 5: (2,), 7: (3,)}
+
+    def pass_on(step, send, *blocks):
         for piece in range(PIECES):
             arrived(step, piece)
             send(step, piece)
             if piece % XS == XS - 1:
                 across(step, piece // XS).start()
+            if blocks and piece in work_after:
+                compute(work_after[piece], *blocks)
 
     def to_next(step, piece):
         forward(step, piece).start()
@@ -292,9 +298,8 @@
             across(step, part).wait_recv()
 
     def turn(step, _):
-        pass_on(step, to_next)
-        crossed(step - 1)
-        compute(sib.at[step - 1], kv.at[step])
+        crossed(step - 2)
+        pass_on(step, to_next, sib.at[step - 2], kv.at[step - 1])
         return 0
 
     pass_on(0, to_next)
@@ -306,13 +311,14 @@
         query(0).wait_recv()
 
     near_across().wait_recv()
-    compute(near, kv.at[0])
-    lax.fori_loop(1, HALF - 2, turn, 0)
-    pass_on(HALF - 2, to_both)
+    pass_on(1, to_next, near, kv.at[0])
+    lax.fori_loop(2, HALF - 2, turn, 0)
+    crossed(HALF - 4)
+    pass_on(HALF - 2, to_both, sib.at[HALF - 4], kv.at[HALF - 3])
     crossed(HALF - 3)
-    compute(sib.at[HALF - 3], kv.at[HALF - 2])
+    compute(range(YS), sib.at[HALF - 3], kv.at[HALF - 2])
     crossed(HALF - 2)
-    compute(sib.at[HALF - 2])
+    compute(range(YS), sib.at[HALF - 2])
     for piece in range(PIECES):
         pltpu.make_async_remote_copy(
             src_ref=far.at[piece],

time: 57.8 us -> 56.8 us (0.983)
  Pallas kernels: 56.2 us -> 55.2 us
    pallas_call x1, Pallas kernels: 56.2 us -> 55.2 us  [local(): pl.pallas_call(kernel, out_shape=jax.ShapeDtypeStruct((ROWS, GROUP * HS),...]
where the time goes in v5:
time: 56.8 us; the launch traced here: 56.6 us
  Pallas kernels  55.2 us (97%)
  local copies, waits for them, and re-layouts  1.42 us (2%)
    pallas_call x1, Pallas kernels, local(): pl.pallas_call(kernel, out_shape=jax.ShapeDtypeStruct((ROWS, GROUP * HS),...  55.2 us
    unnamed x1, local copies, waits for them, and re-layouts  1.42 us

profile of v5, /device:TPU:1, one launch (start us, length us, event | category | flops | bytes accessed | tf_op | source)
XLA Modules:
  0.0 56.6 jit_solution(15093087173345823650)
XLA Ops:
  0.0 55.2 %shard_map.55 = bf16[16,1536]{1,0:T(8,128)(2,1)} custom-call(bf16[16,6144]{1,0:T(8,128)(2,1)} %q_hbm.1, bf16[60,512]{1,0:T(8,128)(2,1)} %k_hbm.1, bf16[60,512]{1,0:T(8,128)(2,1)} %v_hbm.1, bf16[16,128]{1,0:T(8,128)(2,1)} %ok_hbm.1, bf16[16,128]{1,0:T(8,128)(2,1)} %ov_hbm.1), custom_call_target="tpu_custom_call" | custom-call | tf_op jit(solution)/shard_map/pallas_call | solution.py:418
  55.2 1.4 %copy.7 = bf16[16,1536]{1,0:T(8,128)(2,1)} copy(bf16[16,1536]{1,0:T(8,128)(2,1)} %shard_map.55) | data formatting | bytes 98304

commit v6 on v5

--- a/solution.py
+++ b/solution.py
@@ -146,17 +146,6 @@
     fetches[2].wait()
     for h in range(KVH * GROUP):
         qs[h] = q_ref[:, h * HS : (h + 1) * HS]
-    for dy in (2, 1, 3):
-        query(dy).start()
-
-    @pl.when(jnp.logical_not(q_self))
-    def _():
-        query(0).start()
-
-    @pl.when(q_self)
-    def _():
-        qbuf[0] = qs[pl.ds(mine * GROUP, GROUP)]
-
     def forward(step, piece):
         return pltpu.make_async_remote_copy(
             src_ref=kv.at[step, piece],
@@ -270,17 +259,37 @@
     came(2)
     for way in (0, 1):
         relay(way).start()
+    for dy in (2, 1, 3):
+        query(dy).start()
+
+    @pl.when(jnp.logical_not(q_self))
+    def _():
+        query(0).start()
+
+    @pl.when(q_self)
+    def _():
+        qbuf[0] = qs[pl.ds(mine * GROUP, GROUP)]
+
     came(1)
     came(3)
     near_across().start()
+    def left(step):
+        for piece in range(PIECES):
+            forward(step, piece).wait_send()
+        for part in (0, 1):
+            across(step, part).wait_send()
+
     work_after = {1: (0,), 3: (1,), 5: (2,), 7: (3,)}
 
     def pass_on(step, send, *blocks):
         for piece in range(PIECES):
             arrived(step, piece)
             send(step, piece)
-            if piece % XS == XS - 1:
-                across(step, piece // XS).start()
+            if piece == PIECES - 1:
+                for part in (0, 1):
+                    across(step, part).start()
+            if blocks and piece == PIECES - 1:
+                left(step - 1)
             if blocks and piece in work_after:
                 compute(work_after[piece], *blocks)
 
@@ -312,6 +321,19 @@
 
     near_across().wait_recv()
     pass_on(1, to_next, near, kv.at[0])
+    for dx in (1, 2, 3):
+        here(dx).wait_send()
+    for way in (0, 1):
+        relay(way).wait_send()
+        for dx in (1, 3, 0):
+            first(way, dx).wait_send()
+    for dy in (1, 2, 3):
+        query(dy).wait_send()
+
+    @pl.when(jnp.logical_not(q_self))
+    def _():
+        query(0).wait_send()
+
     lax.fori_loop(2, HALF - 2, turn, 0)
     crossed(HALF - 4)
     pass_on(HALF - 2, to_both, sib.at[HALF - 4], kv.at[HALF - 3])
@@ -354,36 +376,13 @@
         omsg[dy, GROUP] = stats.astype(jnp.bfloat16)
         result(dy).start()
 
-    for dx in (1, 2, 3):
-        here(dx).wait_send()
-    for way in (0, 1):
-        relay(way).wait_send()
-        for dx in (1, 3, 0):
-            first(way, dx).wait_send()
-    for dy in (1, 2, 3):
-        query(dy).wait_send()
-
-    @pl.when(jnp.logical_not(q_self))
-    def _():
-        query(0).wait_send()
-
-    def sent(step, _):
-        for piece in range(PIECES):
-            forward(step, piece).wait_send()
-        return 0
-
-    lax.fori_loop(0, HALF - 2, sent, 0)
     for i in range(XS):
         for core in (0, 1):
             last(i, i, core).wait_send()
     near_across().wait_send()
 
-    def across_sent(step, _):
-        for part in (0, 1):
-            across(step, part).wait_send()
-        return 0
-
-    lax.fori_loop(0, HALF - 1, across_sent, 0)
+    for part in (0, 1):
+        across(HALF - 2, part).wait_send()
 
     for dy in range(YS):
         result(dy).wait_recv()

time: 56.8 us -> 56.9 us (level)
  no operation moved by 1% of the time
where the time goes in v6:
time: 56.9 us; the launch traced here: 56.7 us
  Pallas kernels  55.2 us (97%)
  local copies, waits for them, and re-layouts  1.42 us (2%)
    pallas_call x1, Pallas kernels, local(): pl.pallas_call(kernel, out_shape=jax.ShapeDtypeStruct((ROWS, GROUP * HS),...  55.2 us
    unnamed x1, local copies, waits for them, and re-layouts  1.42 us

profile of v6, /device:TPU:1, one launch (start us, length us, event | category | flops | bytes accessed | tf_op | source)
XLA Modules:
  0.0 56.7 jit_solution(9517870014655930973)
XLA Ops:
  0.0 55.2 %shard_map.55 = bf16[16,1536]{1,0:T(8,128)(2,1)} custom-call(bf16[16,6144]{1,0:T(8,128)(2,1)} %q_hbm.1, bf16[60,512]{1,0:T(8,128)(2,1)} %k_hbm.1, bf16[60,512]{1,0:T(8,128)(2,1)} %v_hbm.1, bf16[16,128]{1,0:T(8,128)(2,1)} %ok_hbm.1, bf16[16,128]{1,0:T(8,128)(2,1)} %ov_hbm.1), custom_call_target="tpu_custom_call" | custom-call | tf_op jit(solution)/shard_map/pallas_call | solution.py:417
  55.2 1.4 %copy.7 = bf16[16,1536]{1,0:T(8,128)(2,1)} copy(bf16[16,1536]{1,0:T(8,128)(2,1)} %shard_map.55) | data formatting | bytes 98304
